TPU v7x, 256 devices: a whole 4x4x8 slice. The times are simulated.
256 devices in a mesh: section: 2 (over y_hi), ctx: 128 (over x, y_lo, z, core).
Axes of the slice: x: 4, y: 4 (y_hi: 2, y_lo: 2; y = y_hi * 2 + y_lo), z: 8, core: 2. Of those that a mesh axis runs over, the one named last changes fastest.
Arguments:
- queries: bfloat16 [32768, 2048], P(('section', 'ctx')), parts along dimension 0, may hold values from -300 to 300
- key_rows_slotted: bfloat16 [32768, 512], P(('section', 'ctx')), parts along dimension 0, may hold values from -12 to 12
- value_rows_slotted: bfloat16 [32768, 512], P(('section', 'ctx')), parts along dimension 0, may hold values from -5 to 5
- output_gradient: bfloat16 [32768, 2048], P(('section', 'ctx')), parts along dimension 0, may hold values from -5 to 5
- slot_to_block: int32 [512], P('section'), parts along dimension 0, may hold values from 0 to 255, as said below
- doc_starts: int32 [684], P('section'), parts along dimension 0, may hold values from 0 to 16384, as said below
- block_live: int32 [512, 4], P('section'), parts along dimension 0, may hold values from 0 to 1, as said below
Outputs:
- query_grad: bfloat16 [32768, 2048], P(('section', 'ctx')), parts along dimension 0
- key_gradient: bfloat16 [32768, 512], P(('section', 'ctx')), parts along dimension 0
- value_gradient: bfloat16 [32768, 512], P(('section', 'ctx')), parts along dimension 0
There are 2 independent parts, one for each index of `section`. A program takes and returns all parts, laid end to end along the dimension named above; each array names one. Nothing has to cross between parts.
Inputs may be any that keep to these rules, and one draw needn't show every extreme that they name: `slot_to_block`: index i of ctx holds slots 2i and 2i + 1; slot 2i holds block m and slot 2i + 1 holds block 255 - m, where m = (i - r) mod (128) for one r of each draw. `doc_starts`: Ascending, the first entry 0; every document holds at most 192 tokens; entries equal to 16384 start no document. `block_live`: entry [b, d] is 1 where block b and block b - d of the sequence hold tokens of one document, always 1 at d = 0, else 0.
All inputs are finite; a program needn't handle non-finite values.
Results may differ from a plain program's by a relative error of at most 0.005.
Values may be sent and summed in bfloat16 or wider, within the bound.
No kernel may reach another device: no remote copies, remote signals or barrier semaphores. Data moves between devices by JAX's collectives and lax.ppermute only.
A program may use at most 128 MiB of HBM per device.

v0:
```python
import functools
import math

import jax
import jax.numpy as jnp
from jax import lax
from jax.experimental import pallas as pl
from jax.experimental.pallas import tpu as pltpu
from jax.sharding import PartitionSpec as P

QUERY_HEADS = 16
KEY_VALUE_HEADS = 4
GROUP = QUERY_HEADS // KEY_VALUE_HEADS
HEAD_WIDTH = 128
ROWS = 64
KV = KEY_VALUE_HEADS * HEAD_WIDTH
WIDE = QUERY_HEADS * HEAD_WIDTH
REACH = 3
SPAN = (REACH + 1) * ROWS
SCALE = 1.0 / math.sqrt(HEAD_WIDTH)
EXP2_SCALE = SCALE * math.log2(math.e)
MASKED = -1e30
FAR = 1 << 30
ENTRIES = 7
VMEM_LIMIT = 24 * 1024 * 1024

TABLE_A, TABLE_B, TABLE_C = 4, 5, 6
NEAR_COST = 1 << 34


def send(array, even_by, odd_by):
    count = lax.axis_size("ctx")
    steps = [odd_by if i % 2 else even_by for i in range(count)]
    pairs = [(i, (i + by) % count) for i, by in enumerate(steps) if by is not None]
    return lax.ppermute(array, "ctx", pairs)


def fold_flags(chip_base, slots, live):
    half = slots.shape[0] // 2
    middle_even = slots[chip_base] == half - 1
    middle_odd = slots[chip_base + 2] == half - 1
    far_middle = jnp.logical_and(middle_odd, live[REACH, half] == 1)
    return middle_even, far_middle


def attention_kernel(
    leading,
    place,
    slots,
    live,
    row_start,
    q_own,
    q_sib,
    g_own,
    g_sib,
    kv_own,
    kv_sib,
    kv_a,
    kv_b,
    *refs,
):
    if leading:
        dq, total, table, q_work, g_work, bias = refs
    else:
        kv_c, dq_in, total_in = refs[:3]
        dq_own, out_own, out_sib, out_a, out_b, out_c = refs[3:9]
        dq, total, table, q_work, g_work, bias = refs[9:]
    me = place[0]
    count = slots.shape[0] // 2
    parity = lax.rem(me, 2)
    is_odd = parity == 1
    chip_base = 2 * (me - parity)
    middle_even, far_middle = fold_flags(chip_base, slots, live)

    own_at = pl.multiple_of(parity * 128, 128)
    sib_at = pl.multiple_of((1 - parity) * 128, 128)
    table[pl.ds(own_at, 128), :] = kv_own[...]
    table[pl.ds(sib_at, 128), :] = kv_sib[...]
    table[TABLE_A * ROWS : TABLE_B * ROWS, :] = kv_a[...]
    table[TABLE_B * ROWS : TABLE_C * ROWS, :] = kv_b[...]

    toward = jnp.where(is_odd, 1, -1)
    near_a = lax.rem(me + 2 * toward + count, count)
    near_b = lax.rem(me + toward + count, count)
    far = lax.rem(me + 3 * toward + count, count)
    passed_odd = jnp.logical_and(is_odd, slots[2 * near_a] == count - 1)
    passed_even = jnp.logical_and(is_odd, slots[2 * near_b] == count - 1)
    entry_ids = [slots[chip_base + e] for e in range(4)]
    entry_ids += [slots[2 * near_a + parity], slots[2 * near_b + parity]]
    if not leading:
        table[TABLE_C * ROWS :, :] = kv_c[...]
        passed_middle = jnp.logical_or(passed_odd, passed_even)
        entry_ids += [jnp.where(passed_middle, count - 1, slots[2 * far + parity])]

    own_row = pl.multiple_of(parity * ROWS, ROWS)
    other_row = pl.multiple_of((1 - parity) * ROWS, ROWS)
    other_entry = jnp.where(middle_even, 1 + parity, jnp.where(is_odd, 1, 2))
    slot = 0 if leading else 1

    @pl.when(middle_even)
    def _():
        q_work[slot] = q_own[pl.ds(other_row, ROWS), :]
        g_work[slot] = g_own[pl.ds(other_row, ROWS), :]

    @pl.when(jnp.logical_not(middle_even))
    def _():
        q_work[slot] = q_sib[pl.ds(own_row, ROWS), :]
        g_work[slot] = g_sib[pl.ds(own_row, ROWS), :]

    if leading:
        total[...] = jnp.zeros_like(total)

        @pl.when(far_middle)
        def _():
            q_work[1] = q_sib[ROWS:, :]
            g_work[1] = g_sib[ROWS:, :]

        entries = (other_entry, 3)
        first = jnp.where(passed_even, 1, 0)
        last = jnp.where(jnp.logical_and(far_middle, jnp.logical_not(is_odd)), 2, 1)
    else:
        total[...] = total_in[...]
        q_work[0] = q_own[pl.ds(own_row, ROWS), :]
        g_work[0] = g_own[pl.ds(own_row, ROWS), :]
        entries = (3 * parity, other_entry)
        first = jnp.where(jnp.logical_and(far_middle, is_odd), 1, 0)
        last = jnp.where(passed_even, 2, 1)

    def work_item(item, carry):
        entry = jnp.where(item == 0, *entries)
        query_id = slots[chip_base + entry]
        indices = []
        key_base = []
        for distance in range(REACH + 1):
            key_id = query_id - distance
            is_live = jnp.logical_and(key_id >= 0, live[distance, query_id] == 1)
            index = jnp.int32(0)
            found = jnp.bool_(False)
            for e in range(len(entry_ids)):
                match = entry_ids[e] == key_id
                index = jnp.where(match, e, index)
                found = jnp.logical_or(found, match)
            ok = jnp.logical_and(is_live, found)
            indices.append(pl.multiple_of(jnp.where(ok, index, 0) * ROWS, ROWS))
            key_base.append(jnp.where(ok, key_id * ROWS, FAR))
        lane = lax.broadcasted_iota(jnp.int32, (1, GROUP * ROWS), 1)
        query_pos = query_id * ROWS + lax.rem(lane, ROWS)
        query_start = row_start[pl.ds(entry, 1), :]
        sub = lax.broadcasted_iota(jnp.int32, (ROWS, GROUP * ROWS), 0)
        for distance in range(REACH + 1):
            key_pos = sub + key_base[distance]
            allowed = jnp.logical_and(key_pos <= query_pos, key_pos >= query_start)
            bias[distance * ROWS : (distance + 1) * ROWS, :] = jnp.where(
                allowed, 0.0, MASKED
            )
        for g in range(KEY_VALUE_HEADS):
            kcols = slice(g * HEAD_WIDTH, (g + 1) * HEAD_WIDTH)
            vcols = slice(KV + g * HEAD_WIDTH, KV + (g + 1) * HEAD_WIDTH)
            heads = [
                slice((GROUP * g + j) * HEAD_WIDTH, (GROUP * g + j + 1) * HEAD_WIDTH)
                for j in range(GROUP)
            ]
            keys = jnp.concatenate([table[pl.ds(i, ROWS), kcols] for i in indices], 0)
            values = jnp.concatenate([table[pl.ds(i, ROWS), vcols] for i in indices], 0)
            q = jnp.concatenate([q_work[item, :, h] for h in heads], 0)
            grad = jnp.concatenate([g_work[item, :, h] for h in heads], 0)
            nt = (((1,), (1,)), ((), ()))
            raw = lax.dot_general(keys, q, nt, preferred_element_type=jnp.float32)
            raw = raw + bias[...]
            top = jnp.max(raw, axis=0, keepdims=True)
            weights = jnp.exp2((raw - top) * EXP2_SCALE)
            probs = weights * (1.0 / jnp.sum(weights, axis=0, keepdims=True))
            grad_scores = lax.dot_general(
                values, grad, nt, preferred_element_type=jnp.float32
            )
            offset = jnp.sum(probs * grad_scores, axis=0, keepdims=True)
            score_low = (probs * (grad_scores - offset)).astype(jnp.bfloat16)
            value_add = jnp.dot(
                probs.astype(jnp.bfloat16), grad, preferred_element_type=jnp.float32
            )
            key_add = jnp.dot(score_low, q, preferred_element_type=jnp.float32)
            query_add = lax.dot_general(
                score_low,
                keys,
                (((0,), (0,)), ((), ())),
                preferred_element_type=jnp.float32,
            )
            query_add = (query_add * SCALE).astype(jnp.bfloat16)
            for j, h in enumerate(heads):
                dq[item, :, h] = query_add[j * ROWS : (j + 1) * ROWS]
            for distance in range(REACH + 1):
                part = slice(distance * ROWS, (distance + 1) * ROWS)
                at = pl.ds(indices[distance], ROWS)
                total[at, kcols] += key_add[part] * SCALE
                total[at, vcols] += value_add[part]
        return carry

    lax.fori_loop(first, last, work_item, 0)
    if leading:
        return
    low = jnp.bfloat16
    dq_own[0] = dq[0]
    dq_own[1] = dq_in[0]

    @pl.when(passed_even)
    def _():
        dq_own[1] = dq[1]

    out_sib[:ROWS, :] = dq_own[1]
    out_sib[ROWS : 2 * ROWS, :] = dq_in[1]
    out_sib[2 * ROWS :, : 2 * KV] = total[pl.ds(sib_at, ROWS), :].astype(low)
    out_sib[2 * ROWS :, 2 * KV :] = total[pl.ds(sib_at + ROWS, ROWS), :].astype(low)
    out_own[...] = total[pl.ds(own_at, 128), :]
    out_a[:ROWS, :] = total[TABLE_A * ROWS : TABLE_B * ROWS, :].astype(low)
    out_b[...] = total[TABLE_B * ROWS : TABLE_C * ROWS, :].astype(low)
    passed = total[TABLE_C * ROWS :, :].astype(low)
    out_a[ROWS:, :] = jnp.zeros_like(passed)
    out_c[...] = passed

    @pl.when(passed_middle)
    def _():
        out_a[ROWS:, :] = passed
        out_c[...] = jnp.zeros_like(passed)


def pack_kernel(
    place,
    slots_hbm,
    docs_hbm,
    keys,
    values,
    queries,
    grads,
    both,
    chain,
    cross,
    q_own,
    g_own,
    row_start,
    fold,
    slots,
    docs,
    sems,
):
    parity = lax.rem(place[0], 2)
    own_rows = pl.ds(pl.multiple_of(parity * ROWS, ROWS), ROWS)
    other_rows = pl.ds(pl.multiple_of((1 - parity) * ROWS, ROWS), ROWS)
    copies = [
        pltpu.make_async_copy(source, target, sems.at[n])
        for n, (source, target) in enumerate(
            [
                (slots_hbm, slots),
                (docs_hbm, docs),
                (keys.at[other_rows, :], cross.at[:, pl.ds(0, KV)]),
                (values.at[other_rows, :], cross.at[:, pl.ds(KV, KV)]),
                (keys.at[own_rows, :], chain.at[:, pl.ds(0, KV)]),
                (values.at[own_rows, :], chain.at[:, pl.ds(KV, KV)]),
                (keys, both.at[:, pl.ds(0, KV)]),
                (values, both.at[:, pl.ds(KV, KV)]),
                (queries, q_own),
                (grads, g_own),
            ]
        )
    ]
    for copy in copies:
        copy.start()
    copies[0].wait()
    copies[1].wait()
    middle = slots.shape[0] // 2 - 1
    chip_base = 2 * (place[0] - parity)
    holder = jnp.where(
        slots[chip_base + 2] == middle, 1, jnp.where(slots[chip_base] == middle, 2, 0)
    )
    fold[...] = jnp.full(fold.shape, jnp.where(parity == 1, holder, 0).astype(jnp.float32))
    count = docs.shape[0]
    lane = lax.rem(lax.broadcasted_iota(jnp.int32, (1, GROUP * ROWS), 1), ROWS)
    for entry in range(4):
        first = slots[chip_base + entry] * ROWS

        def halve(_, bounds):
            low, high = bounds
            middle = (low + high) // 2
            begun = docs[middle] <= first
            inside = low < high
            return (
                jnp.where(jnp.logical_and(inside, begun), middle + 1, low),
                jnp.where(jnp.logical_and(inside, jnp.logical_not(begun)), middle, high),
            )

        begun, _ = lax.fori_loop(
            0, count.bit_length(), halve, (jnp.int32(1), jnp.int32(count))
        )

        def more(state):
            index, _ = state
            start = docs[jnp.minimum(index, count - 1)]
            return jnp.logical_and(index < count, start < first + ROWS)

        def step(state):
            index, row = state
            start = docs[index]
            return index + 1, jnp.where(lane + first >= start, start, row)

        _, row = lax.while_loop(
            more, step, (begun, jnp.full((1, GROUP * ROWS), docs[begun - 1]))
        )
        row_start[pl.ds(entry, 1), :] = row
    for copy in copies[2:]:
        copy.wait()


def near_kernel(place, slots, own, back_a, out):
    parity = lax.rem(place[0], 2)
    is_odd = parity == 1
    own_rows = pl.ds(pl.multiple_of(parity * ROWS, ROWS), ROWS)
    out[...] = own[...]
    out[own_rows, :] += back_a[:ROWS, :].astype(jnp.float32)
    holder = slots[2 * (place[0] - parity) + 2] == slots.shape[0] // 2 - 1

    @pl.when(jnp.logical_and(is_odd, holder))
    def _():
        out[:ROWS, :] += back_a[ROWS:, :].astype(jnp.float32)


def final_kernel(place, slots, live, mine, own, lent, back_c, back_b, theirs, *outs):
    query_out, key_out, value_out = outs
    me = place[0]
    parity = lax.rem(me, 2)
    is_odd = parity == 1
    chip_base = 2 * (me - parity)
    middle_even, far_middle = fold_flags(chip_base, slots, live)
    own_rows = pl.ds(pl.multiple_of(parity * ROWS, ROWS), ROWS)
    other_rows = pl.ds(pl.multiple_of((1 - parity) * ROWS, ROWS), ROWS)
    moved = jnp.logical_and(far_middle, is_odd)

    @pl.when(moved)
    def _():
        query_out[own_rows, :] = theirs[ROWS : 2 * ROWS, :]

    @pl.when(jnp.logical_not(moved))
    def _():
        query_out[own_rows, :] = mine[0]

    @pl.when(middle_even)
    def _():
        query_out[other_rows, :] = mine[1]

    @pl.when(jnp.logical_not(middle_even))
    def _():
        query_out[other_rows, :] = theirs[:ROWS, :]

    f32 = jnp.float32
    for out, first in ((key_out, 0), (value_out, KV)):
        columns = slice(first, first + KV)
        cross = back_b[:, columns].astype(f32) + back_c[:, columns].astype(f32)
        low = own[:ROWS, columns] + theirs[2 * ROWS :, columns].astype(f32)
        low = low + lent[:, columns].astype(f32) + jnp.where(is_odd, cross, 0.0)
        high = own[ROWS:, columns] + theirs[2 * ROWS :, 2 * KV + first : 3 * KV + first].astype(f32)
        out[:ROWS, :] = low.astype(out.dtype)
        out[ROWS:, :] = (high + jnp.where(is_odd, 0.0, cross)).astype(out.dtype)


def vmem(count):
    return [pl.BlockSpec(memory_space=pltpu.VMEM)] * count


def in_hbm(array):
    return pltpu.with_memory_space_constraint(array, pltpu.HBM)


def hbm(count):
    return [pl.BlockSpec(memory_space=pltpu.HBM)] * count


def smem(count):
    return [pl.BlockSpec(memory_space=pltpu.SMEM)] * count


def shards(
    queries,
    key_rows_slotted,
    value_rows_slotted,
    output_gradient,
    slot_to_block,
    doc_starts,
    block_live,
):
    me = lax.axis_index("ctx")
    place = me.astype(jnp.int32).reshape(1)
    live = block_live.T
    params = pltpu.CompilerParams(vmem_limit_bytes=VMEM_LIMIT)

    bf16 = functools.partial(jax.ShapeDtypeStruct, dtype=jnp.bfloat16)
    kv, kv_chain, kv_cross, q_own, g_own, row_start, fold = pl.pallas_call(
        pack_kernel,
        out_shape=(
            bf16((2 * ROWS, 2 * KV)),
            bf16((ROWS, 2 * KV)),
            bf16((ROWS, 2 * KV)),
            bf16((2 * ROWS, WIDE)),
            bf16((2 * ROWS, WIDE)),
            jax.ShapeDtypeStruct((4, GROUP * ROWS), jnp.int32),
            jax.ShapeDtypeStruct((ROWS, 2 * KV), jnp.float32),
        ),
        in_specs=smem(1) + hbm(6),
        out_specs=tuple(vmem(7)),
        scratch_shapes=[
            pltpu.SMEM(slot_to_block.shape, jnp.int32),
            pltpu.SMEM(doc_starts.shape, jnp.int32),
            pltpu.SemaphoreType.DMA((10,)),
        ],
        compiler_params=params,
        name="prepare",
    )(
        place,
        in_hbm(slot_to_block),
        in_hbm(doc_starts),
        in_hbm(key_rows_slotted),
        in_hbm(value_rows_slotted),
        in_hbm(queries),
        in_hbm(output_gradient),
    )
    kv_a = send(kv_chain, 2, -2)
    kv_b = send(kv_cross, -1, 1)
    kv_sib = send(kv, 1, -1)
    q_sib = send(queries, 1, -1)
    g_sib = send(output_gradient, 1, -1)
    passed = jnp.where(fold == 1, kv[:ROWS], jnp.where(fold == 2, kv_sib[:ROWS], kv_b))
    kv_c = send(passed, 2, -2)

    work = [
        pltpu.VMEM((2, ROWS, WIDE), jnp.bfloat16),
        pltpu.VMEM((ENTRIES * ROWS, 2 * KV), jnp.bfloat16),
        pltpu.VMEM((2, ROWS, WIDE), jnp.bfloat16),
        pltpu.VMEM((2, ROWS, WIDE), jnp.bfloat16),
        pltpu.VMEM((SPAN, GROUP * ROWS), jnp.float32),
    ]
    sums = jax.ShapeDtypeStruct((ENTRIES * ROWS, 2 * KV), jnp.float32)
    operands = (
        place,
        in_hbm(slot_to_block),
        live,
        row_start,
        q_own,
        q_sib,
        g_own,
        g_sib,
        kv,
        kv_sib,
        kv_a,
        kv_b,
    )
    dq_leading, total = pl.pallas_call(
        functools.partial(attention_kernel, True),
        out_shape=(bf16((2, ROWS, WIDE)), sums),
        in_specs=smem(3) + vmem(9),
        out_specs=tuple(vmem(2)),
        scratch_shapes=work[1:],
        compiler_params=params,
        cost_estimate=pl.CostEstimate(
            flops=1 << 36, bytes_accessed=1 << 22, transcendentals=1 << 18
        ),
        name="attention_leading",
    )(*operands)
    wide = jax.ShapeDtypeStruct((2 * ROWS, 2 * KV), jnp.float32)
    dq_own, own, out_sib, out_a, out_b, out_c = pl.pallas_call(
        functools.partial(attention_kernel, False),
        out_shape=(
            bf16((2, ROWS, WIDE)),
            wide,
            bf16((3 * ROWS, WIDE)),
            bf16((2 * ROWS, 2 * KV)),
            bf16((ROWS, 2 * KV)),
            bf16((ROWS, 2 * KV)),
        ),
        in_specs=smem(3) + vmem(12),
        out_specs=tuple(vmem(6)),
        scratch_shapes=work[:1] + [pltpu.VMEM(sums.shape, jnp.float32)] + work[1:],
        compiler_params=params,
        name="attention_last",
    )(*operands, kv_c, dq_leading, total)

    back_a = send(out_a, -2, 2)
    back_c = send(out_c, -3, 3)
    back_b = send(out_b, -1, 1)
    back_sib = send(out_sib, 1, -1)
    lent = send(jnp.where(fold == 2, back_a[ROWS:], 0), None, -1)

    own = pl.pallas_call(
        near_kernel,
        out_shape=wide,
        in_specs=smem(2) + vmem(2),
        out_specs=vmem(1)[0],
        compiler_params=params,
        cost_estimate=pl.CostEstimate(
            flops=NEAR_COST, bytes_accessed=1 << 20, transcendentals=0
        ),
        name="two_away_sum",
    )(place, in_hbm(slot_to_block), own, back_a)

    query_grad, key_gradient, value_gradient = pl.pallas_call(
        final_kernel,
        out_shape=(bf16((2 * ROWS, WIDE)), bf16((2 * ROWS, KV)), bf16((2 * ROWS, KV))),
        in_specs=smem(3) + vmem(6),
        out_specs=tuple(vmem(3)),
        scratch_shapes=[],
        compiler_params=params,
        name="gradients_out",
    )(
        place,
        in_hbm(slot_to_block),
        live,
        dq_own,
        own,
        lent,
        back_c,
        back_b,
        back_sib,
    )
    return query_grad, key_gradient, value_gradient


def solution(mesh):
    rows = P(("section", "ctx"), None)
    return jax.shard_map(
        shards,
        mesh=mesh,
        in_specs=(rows, rows, rows, rows, P("section"), P("section"), P("section", None)),
        out_specs=(rows, rows, rows),
        check_vma=False,
    )
```

profile of v0, /device:TPU:16, one launch (start us, length us, event | category | flops | bytes accessed | tf_op | source)
XLA Modules:
  0.0 43.9 jit_solution(14890814941803609678)
XLA Ops:
  0.6 0.0 copy-start
  0.6 0.1 collective-permute-start
  0.7 0.5 %collective-permute-start.1 = (bf16[128,2048]{1,0:T(8,128)(2,1)}, bf16[128,2048]{1,0:T(8,128)(2,1)S(1)}, u32[]{:S(2)}, u32[]{:S(2)}) collective-permute-start(bf16[128,2048]{1,0:T(8,128)(2,1)} %grads.1), channel_id=1, source_target_pairs={{0,1},{1,0},{2,3},{3,2},{4,5},{5,4},{6,7},{7,6},{8,9},{9,8},{10,11... | collective-permute-start | bytes 1572872 | tf_op jit(solution)/shard_map/ppermute | solution.py:35
  1.2 1.6 %prepare.1 = (bf16[128,1024]{1,0:T(8,128)(2,1)S(1)}, bf16[64,1024]{1,0:T(8,128)(2,1)S(1)}, bf16[64,1024]{1,0:T(8,128)(2,1)S(1)}, bf16[128,2048]{1,0:T(8,128)(2,1...) custom-call(s32[1]{0:T(128)} %bitcast.place, s32[256]{0:T(256)} %slots.7, ...), custom_call_target="tpu_custom_call" | custom-call | tf_op jit(solution)/shard_map/prepare/pallas_call | solution.py:394
  2.8 0.2 collective-permute-start.2
  3.0 8.8 %collective-permute-start.4 = (bf16[64,1024]{1,0:T(8,128)(2,1)S(1)}, bf16[64,1024]{1,0:T(8,128)(2,1)S(1)}, u32[]{:S(2)}, u32[]{:S(2)}) collective-permute-start(bf16[64,1024]{1,0:T(8,128)(2,1)S(1)} %get-tuple-element.23), channel_id=1, source_target_pairs={{0,127},{1,2},{2,1},{3,4},{4,3},{5,6},{6,5},{7,8},{8,7},{9,10},{10... | collective-permute-start | bytes 393224 | tf_op jit(solution)/shard_map/ppermute | solution.py:35
  11.8 0.0 collective-permute-start.3
  11.8 3.3 %collective-permute-done.4.kv_b = bf16[64,1024]{1,0:T(8,128)(2,1)S(1)} collective-permute-done((bf16[64,1024]{1,0:T(8,128)(2,1)S(1)}, bf16[64,1024]{1,0:T(8,128)(2,1)S(1)}, u32[]{:S(2)}, u32[]{:S(2)}) %collective-permute-start.4) | collective-permute-done | bytes 131104 | tf_op jit(solution)/shard_map/ppermute | solution.py:35
  15.1 0.0 collective-permute-done.2.kv_sib
  15.1 0.1 compare_select_fusion
  15.2 0.1 collective-permute-start.5
  15.3 5.7 %collective-permute-done.3.kv_a = bf16[64,1024]{1,0:T(8,128)(2,1)S(1)} collective-permute-done((bf16[64,1024]{1,0:T(8,128)(2,1)S(1)}, bf16[64,1024]{1,0:T(8,128)(2,1)S(1)}, u32[]{:S(2)}, u32[]{:S(2)}) %collective-permute-start.3) | collective-permute-done | bytes 131104 | tf_op jit(solution)/shard_map/ppermute | solution.py:35
  21.0 0.0 collective-permute-done.q_sib
  21.0 0.0 collective-permute-done.1.g_sib
  21.0 0.0 copy-done
  21.0 2.7 %attention_leading.1 = (bf16[2,64,2048]{2,1,0:T(8,128)(2,1)S(1)}, f32[448,1024]{1,0:T(8,128)S(1)}) custom-call(s32[1]{0:T(128)} %bitcast.place, s32[256]{0:T(256)} %slots.7, s32[4,256]{1,0:T(4,128)S(1)} %bitcast.2, s32[4,256]{1,0:T(4,128)S(1)} %get-tuple-element.18.row_start, bf16[128,2048]{1,0:T(8,128)(2,1)S(1)} %get-tuple-element.19.q_own, ...), custom_call_target="tpu_custom_call" | custom-call | flops 68719476736 | bytes 4194304 | tf_op jit(solution)/shard_map/attention_leading/pallas_call | solution.py:453
  23.7 0.8 %collective-permute-done.5.refs_0_ = bf16[64,1024]{1,0:T(8,128)(2,1)S(1)} collective-permute-done((bf16[64,1024]{1,0:T(8,128)(2,1)S(1)}, bf16[64,1024]{1,0:T(8,128)(2,1)S(1)}, u32[]{:S(2)}, u32[]{:S(2)}) %collective-permute-start.5) | collective-permute-done | bytes 131104 | tf_op jit(solution)/shard_map/ppermute | solution.py:35
  24.5 2.9 %attention_last.1 = (bf16[2,64,2048]{2,1,0:T(8,128)(2,1)S(1)}, f32[128,1024]{1,0:T(8,128)S(1)}, bf16[192,2048]{1,0:T(8,128)(2,1)S(1)}, bf16[128,1024]{1,0:T(8,12...) custom-call(s32[1]{0:T(128)} %bitcast.place, s32[256]{0:T(256)} %slots.7, s32[4,256]{1,0:T(4,128)S(1)} %bitcast.3, ...), custom_call_target="tpu_custom_call" | custom-call | tf_op jit(solution)/shard_map/attention_last/pallas_call | solution.py:466
  27.4 0.1 collective-permute-start.6
  27.5 6.1 %collective-permute-start.8 = (bf16[64,1024]{1,0:T(8,128)(2,1)S(1)}, bf16[64,1024]{1,0:T(8,128)(2,1)S(1)}, u32[]{:S(2)}, u32[]{:S(2)}) collective-permute-start(bf16[64,1024]{1,0:T(8,128)(2,1)S(1)} %get-tuple-element.30), channel_id=1, source_target_pairs={{0,125},{1,4},{2,127},{3,6},{4,1},{5,8},{6,3},{7,10},{8,5},{9,12},... | collective-permute-start | bytes 393224 | tf_op jit(solution)/shard_map/ppermute | solution.py:35
  33.6 1.3 %collective-permute-start.9 = (bf16[64,1024]{1,0:T(8,128)(2,1)S(1)}, bf16[64,1024]{1,0:T(8,128)(2,1)S(1)}, u32[]{:S(2)}, u32[]{:S(2)}) collective-permute-start(bf16[64,1024]{1,0:T(8,128)(2,1)S(1)} %get-tuple-element.31), channel_id=1, source_target_pairs={{0,127},{1,2},{2,1},{3,4},{4,3},{5,6},{6,5},{7,8},{8,7},{9,10},{10... | collective-permute-start | bytes 393224 | tf_op jit(solution)/shard_map/ppermute | solution.py:35
  34.9 0.0 collective-permute-start.10
  34.9 0.3 collective-permute-done.6.back_a
  35.3 1.3 %collective-permute-start.7 = (bf16[64,1024]{1,0:T(8,128)(2,1)S(1)}, bf16[64,1024]{1,0:T(8,128)(2,1)S(1)}, u32[]{:S(2)}, u32[]{:S(2)}) collective-permute-start(bf16[64,1024]{1,0:T(8,128)(2,1)S(1)} %slice_select_fusion), channel_id=1, source_target_pairs={{1,0},{3,2},{5,4},{7,6},{9,8},{11,10},{13,12},{15,14},{17,16},{19,... | collective-permute-start | bytes 393224 | tf_op jit(solution)/shard_map/ppermute | solution.py:35
  36.6 0.8 %two_away_sum.1.own = f32[128,1024]{1,0:T(8,128)S(1)} custom-call(s32[1]{0:T(128)} %bitcast.place, s32[256]{0:T(256)} %slots.7, f32[128,1024]{1,0:T(8,128)S(1)} %get-tuple-element.28.own, bf16[128,1024]{1,0:T(8,128)(2,1)S(1)} %collective-permute-done.6.back_a), custom_call_target="tpu_custom_call" | custom-call | flops 17179869184 | bytes 1048576 | tf_op jit(solution)/shard_map/two_away_sum/pallas_call | solution.py:489
  37.3 2.9 %collective-permute-done.8.back_c = bf16[64,1024]{1,0:T(8,128)(2,1)S(1)} collective-permute-done((bf16[64,1024]{1,0:T(8,128)(2,1)S(1)}, bf16[64,1024]{1,0:T(8,128)(2,1)S(1)}, u32[]{:S(2)}, u32[]{:S(2)}) %collective-permute-start.8) | collective-permute-done | bytes 131104 | tf_op jit(solution)/shard_map/ppermute | solution.py:35
  40.2 2.0 %collective-permute-done.9.back_b = bf16[64,1024]{1,0:T(8,128)(2,1)S(1)} collective-permute-done((bf16[64,1024]{1,0:T(8,128)(2,1)S(1)}, bf16[64,1024]{1,0:T(8,128)(2,1)S(1)}, u32[]{:S(2)}, u32[]{:S(2)}) %collective-permute-start.9) | collective-permute-done | bytes 131104 | tf_op jit(solution)/shard_map/ppermute | solution.py:35
  42.2 0.0 collective-permute-done.7.lent
  42.2 0.0 collective-permute-done.10.theirs
  42.2 1.6 %gradients_out.1 = (bf16[128,2048]{1,0:T(8,128)(2,1)}, bf16[128,512]{1,0:T(8,128)(2,1)}, bf16[128,512]{1,0:T(8,128)(2,1)}) custom-call(s32[1]{0:T(128)} %bitcast.place, s32[256]{0:T(256)} %slots.7, s32[4,256]{1,0:T(4,128)S(1)} %bitcast.4, bf16[2,64,2048]{2,1,0:T(8,128)(2,1)S(1)} %get-tuple-element.27.mine, f32[128,1024]{1,0:T(8,128)S(1)} %two_away_sum.1.own, ...), custom_call_target="tpu_custom_call" | custom-call | tf_op jit(solution)/shard_map/gradients_out/pallas_call | solution.py:501
  (1 shorter events, 0.0 us)
Async XLA Ops:
  0.6 20.3 %copy-start = (s32[256,4]{0,1:T(4,128)S(1)}, s32[256,4]{0,1:T(4,128)}, u32[]{:S(2)}) copy-start(s32[256,4]{0,1:T(4,128)} %param.13) | copy-start | bytes 12292
  0.6 20.3 %collective-permute-start = (bf16[128,2048]{1,0:T(8,128)(2,1)}, bf16[128,2048]{1,0:T(8,128)(2,1)S(1)}, u32[]{:S(2)}, u32[]{:S(2)}) collective-permute-start(bf16[128,2048]{1,0:T(8,128)(2,1)} %queries.1), channel_id=1, source_target_pairs={{0,1},{1,0},{2,3},{3,2},{4,5},{5,4},{6,7},{7,6},{8,9},{9,8},{10,11... | collective-permute-start | bytes 1572872 | tf_op jit(solution)/shard_map/ppermute | solution.py:35
  0.7 20.2 %collective-permute-start.1 = (bf16[128,2048]{1,0:T(8,128)(2,1)}, bf16[128,2048]{1,0:T(8,128)(2,1)S(1)}, u32[]{:S(2)}, u32[]{:S(2)}) collective-permute-start(bf16[128,2048]{1,0:T(8,128)(2,1)} %grads.1), channel_id=1, source_target_pairs={{0,1},{1,0},{2,3},{3,2},{4,5},{5,4},{6,7},{7,6},{8,9},{9,8},{10,11... | collective-permute-start | bytes 1572872 | tf_op jit(solution)/shard_map/ppermute | solution.py:35
  2.8 12.3 %collective-permute-start.2 = (bf16[128,1024]{1,0:T(8,128)(2,1)S(1)}, bf16[128,1024]{1,0:T(8,128)(2,1)S(1)}, u32[]{:S(2)}, u32[]{:S(2)}) collective-permute-start(bf16[128,1024]{1,0:T(8,128)(2,1)S(1)} %get-tuple-element.21.kv_own), channel_id=1, source_target_pairs={{0,1},{1,0},{2,3},{3,2},{4,5},{5,4},{6,7},{7,6},{8,9},{9,8},{10,11... | collective-permute-start | bytes 786440 | tf_op jit(solution)/shard_map/ppermute | solution.py:35
  3.0 12.1 %collective-permute-start.4 = (bf16[64,1024]{1,0:T(8,128)(2,1)S(1)}, bf16[64,1024]{1,0:T(8,128)(2,1)S(1)}, u32[]{:S(2)}, u32[]{:S(2)}) collective-permute-start(bf16[64,1024]{1,0:T(8,128)(2,1)S(1)} %get-tuple-element.23), channel_id=1, source_target_pairs={{0,127},{1,2},{2,1},{3,4},{4,3},{5,6},{6,5},{7,8},{8,7},{9,10},{10... | collective-permute-start | bytes 393224 | tf_op jit(solution)/shard_map/ppermute | solution.py:35
  11.8 9.2 %collective-permute-start.3 = (bf16[64,1024]{1,0:T(8,128)(2,1)S(1)}, bf16[64,1024]{1,0:T(8,128)(2,1)S(1)}, u32[]{:S(2)}, u32[]{:S(2)}) collective-permute-start(bf16[64,1024]{1,0:T(8,128)(2,1)S(1)} %get-tuple-element.22), channel_id=1, source_target_pairs={{0,2},{1,127},{2,4},{3,1},{4,6},{5,3},{6,8},{7,5},{8,10},{9,7},{10... | collective-permute-start | bytes 393224 | tf_op jit(solution)/shard_map/ppermute | solution.py:35
  15.2 9.3 %collective-permute-start.5 = (bf16[64,1024]{1,0:T(8,128)(2,1)S(1)}, bf16[64,1024]{1,0:T(8,128)(2,1)S(1)}, u32[]{:S(2)}, u32[]{:S(2)}) collective-permute-start(bf16[64,1024]{1,0:T(8,128)(2,1)S(1)} %compare_select_fusion), channel_id=1, source_target_pairs={{0,2},{1,127},{2,4},{3,1},{4,6},{5,3},{6,8},{7,5},{8,10},{9,7},{10... | collective-permute-start | bytes 393224 | tf_op jit(solution)/shard_map/ppermute | solution.py:35
  27.4 7.9 %collective-permute-start.6 = (bf16[128,1024]{1,0:T(8,128)(2,1)S(1)}, bf16[128,1024]{1,0:T(8,128)(2,1)S(1)}, u32[]{:S(2)}, u32[]{:S(2)}) collective-permute-start(bf16[128,1024]{1,0:T(8,128)(2,1)S(1)} %get-tuple-element.29), channel_id=1, source_target_pairs={{0,126},{1,3},{2,0},{3,5},{4,2},{5,7},{6,4},{7,9},{8,6},{9,11},{10... | collective-permute-start | bytes 786440 | tf_op jit(solution)/shard_map/ppermute | solution.py:35
  27.5 12.7 %collective-permute-start.8 = (bf16[64,1024]{1,0:T(8,128)(2,1)S(1)}, bf16[64,1024]{1,0:T(8,128)(2,1)S(1)}, u32[]{:S(2)}, u32[]{:S(2)}) collective-permute-start(bf16[64,1024]{1,0:T(8,128)(2,1)S(1)} %get-tuple-element.30), channel_id=1, source_target_pairs={{0,125},{1,4},{2,127},{3,6},{4,1},{5,8},{6,3},{7,10},{8,5},{9,12},... | collective-permute-start | bytes 393224 | tf_op jit(solution)/shard_map/ppermute | solution.py:35
  33.6 8.6 %collective-permute-start.9 = (bf16[64,1024]{1,0:T(8,128)(2,1)S(1)}, bf16[64,1024]{1,0:T(8,128)(2,1)S(1)}, u32[]{:S(2)}, u32[]{:S(2)}) collective-permute-start(bf16[64,1024]{1,0:T(8,128)(2,1)S(1)} %get-tuple-element.31), channel_id=1, source_target_pairs={{0,127},{1,2},{2,1},{3,4},{4,3},{5,6},{6,5},{7,8},{8,7},{9,10},{10... | collective-permute-start | bytes 393224 | tf_op jit(solution)/shard_map/ppermute | solution.py:35
  34.9 7.3 %collective-permute-start.10 = (bf16[192,2048]{1,0:T(8,128)(2,1)S(1)}, bf16[192,2048]{1,0:T(8,128)(2,1)S(1)}, u32[]{:S(2)}, u32[]{:S(2)}) collective-permute-start(bf16[192,2048]{1,0:T(8,128)(2,1)S(1)} %get-tuple-element.32), channel_id=1, source_target_pairs={{0,1},{1,0},{2,3},{3,2},{4,5},{5,4},{6,7},{7,6},{8,9},{9,8},{10,11... | collective-permute-start | bytes 2359304 | tf_op jit(solution)/shard_map/ppermute | solution.py:35
  35.3 7.0 %collective-permute-start.7 = (bf16[64,1024]{1,0:T(8,128)(2,1)S(1)}, bf16[64,1024]{1,0:T(8,128)(2,1)S(1)}, u32[]{:S(2)}, u32[]{:S(2)}) collective-permute-start(bf16[64,1024]{1,0:T(8,128)(2,1)S(1)} %slice_select_fusion), channel_id=1, source_target_pairs={{1,0},{3,2},{5,4},{7,6},{9,8},{11,10},{13,12},{15,14},{17,16},{19,... | collective-permute-start | bytes 393224 | tf_op jit(solution)/shard_map/ppermute | solution.py:35
where the time goes:
time: 44.1 us; the launch traced here: 43.9 us
  starting transfers between devices  18.4 us (42%)
  waiting for transfers between devices  15.1 us (34%)
  Pallas kernels  9.57 us (22%)
  between operations  0.72 us (2%)
    ppermute x11, starting transfers between devices, send(): return lax.ppermute(array, 'ctx', pairs)  18.4 us
    ppermute x11, waiting for transfers between devices, send(): return lax.ppermute(array, 'ctx', pairs)  15.1 us
    pallas_call x1, Pallas kernels, shards(): pl.pallas_call(functools.partial(attention_kernel, False), out_shape=(bf1...  2.92 us
    pallas_call x1, Pallas kernels, shards(): pl.pallas_call(functools.partial(attention_kernel, True), out_shape=(bf16...  2.7 us
    pallas_call x1, Pallas kernels, shards(): pl.pallas_call(final_kernel, out_shape=(bf16((2 * ROWS, WIDE)), bf16((2 *...  1.64 us
    pallas_call x1, Pallas kernels, shards(): pl.pallas_call(pack_kernel, out_shape=(bf16((2 * ROWS, 2 * KV)), bf16((RO...  1.56 us
  transfers between devices with their start and end apart: 11, of which 6 were waited for; matrix products, arithmetic and copies ran while one was open for 0% of the time, Pallas kernels for 11%

commit v1 on v0

--- a/solution.py
+++ b/solution.py
@@ -322,7 +322,7 @@
         out[:ROWS, :] += back_a[ROWS:, :].astype(jnp.float32)
 
 
-def final_kernel(place, slots, live, mine, own, lent, back_c, back_b, theirs, *outs):
+def final_kernel(place, slots, live, mine, own, lent, back_b, back_c, theirs, *outs):
     query_out, key_out, value_out = outs
     me = place[0]
     parity = lax.rem(me, 2)
@@ -513,8 +513,8 @@
         dq_own,
         own,
         lent,
+        back_b,
         back_c,
-        back_b,
         back_sib,
     )
     return query_grad, key_gradient, value_gradient

time: 44.1 us -> 44.2 us (level)
  waiting for transfers between devices: 15.1 us -> 16.4 us
  starting transfers between devices: 18.4 us -> 17.2 us
    ppermute x11, waiting for transfers between devices: 15.1 us -> 16.4 us  [send(): return lax.ppermute(array, 'ctx', pairs)]
    ppermute x11, starting transfers between devices: 18.4 us -> 17.2 us  [send(): return lax.ppermute(array, 'ctx', pairs)]
where the time goes in v1:
time: 44.2 us; the launch traced here: 44 us
  starting transfers between devices  17.2 us (39%)
  waiting for transfers between devices  16.4 us (37%)
  Pallas kernels  9.56 us (22%)
  between operations  0.72 us (2%)
    ppermute x11, starting transfers between devices, send(): return lax.ppermute(array, 'ctx', pairs)  17.2 us
    ppermute x11, waiting for transfers between devices, send(): return lax.ppermute(array, 'ctx', pairs)  16.4 us
    pallas_call x1, Pallas kernels, shards(): pl.pallas_call(functools.partial(attention_kernel, False), out_shape=(bf1...  2.92 us
    pallas_call x1, Pallas kernels, shards(): pl.pallas_call(functools.partial(attention_kernel, True), out_shape=(bf16...  2.69 us
    pallas_call x1, Pallas kernels, shards(): pl.pallas_call(final_kernel, out_shape=(bf16((2 * ROWS, WIDE)), bf16((2 *...  1.64 us
    pallas_call x1, Pallas kernels, shards(): pl.pallas_call(pack_kernel, out_shape=(bf16((2 * ROWS, 2 * KV)), bf16((RO...  1.56 us
  transfers between devices with their start and end apart: 11, of which 6 were waited for; matrix products, arithmetic and copies ran while one was open for 0% of the time, Pallas kernels for 11%

profile of v1, /device:TPU:16, one launch (start us, length us, event | category | flops | bytes accessed | tf_op | source)
XLA Modules:
  0.0 44.0 jit_solution(2613060391001220041)
XLA Ops:
  0.6 0.0 copy-start
  0.6 0.1 collective-permute-start
  0.7 0.5 %collective-permute-start.1 = (bf16[128,2048]{1,0:T(8,128)(2,1)}, bf16[128,2048]{1,0:T(8,128)(2,1)S(1)}, u32[]{:S(2)}, u32[]{:S(2)}) collective-permute-start(bf16[128,2048]{1,0:T(8,128)(2,1)} %grads.1), channel_id=1, source_target_pairs={{0,1},{1,0},{2,3},{3,2},{4,5},{5,4},{6,7},{7,6},{8,9},{9,8},{10,11... | collective-permute-start | bytes 1572872 | tf_op jit(solution)/shard_map/ppermute | solution.py:35
  1.2 1.6 %prepare.1 = (bf16[128,1024]{1,0:T(8,128)(2,1)S(1)}, bf16[64,1024]{1,0:T(8,128)(2,1)S(1)}, bf16[64,1024]{1,0:T(8,128)(2,1)S(1)}, bf16[128,2048]{1,0:T(8,128)(2,1...) custom-call(s32[1]{0:T(128)} %bitcast.place, s32[256]{0:T(256)} %slots.7, ...), custom_call_target="tpu_custom_call" | custom-call | tf_op jit(solution)/shard_map/prepare/pallas_call | solution.py:394
  2.8 0.2 collective-permute-start.2
  3.0 8.8 %collective-permute-start.4 = (bf16[64,1024]{1,0:T(8,128)(2,1)S(1)}, bf16[64,1024]{1,0:T(8,128)(2,1)S(1)}, u32[]{:S(2)}, u32[]{:S(2)}) collective-permute-start(bf16[64,1024]{1,0:T(8,128)(2,1)S(1)} %get-tuple-element.23), channel_id=1, source_target_pairs={{0,127},{1,2},{2,1},{3,4},{4,3},{5,6},{6,5},{7,8},{8,7},{9,10},{10... | collective-permute-start | bytes 393224 | tf_op jit(solution)/shard_map/ppermute | solution.py:35
  11.8 0.0 collective-permute-start.3
  11.8 3.3 %collective-permute-done.4.kv_b = bf16[64,1024]{1,0:T(8,128)(2,1)S(1)} collective-permute-done((bf16[64,1024]{1,0:T(8,128)(2,1)S(1)}, bf16[64,1024]{1,0:T(8,128)(2,1)S(1)}, u32[]{:S(2)}, u32[]{:S(2)}) %collective-permute-start.4) | collective-permute-done | bytes 131104 | tf_op jit(solution)/shard_map/ppermute | solution.py:35
  15.1 0.0 collective-permute-done.2.kv_sib
  15.1 0.1 compare_select_fusion
  15.2 0.1 collective-permute-start.5
  15.3 5.7 %collective-permute-done.3.kv_a = bf16[64,1024]{1,0:T(8,128)(2,1)S(1)} collective-permute-done((bf16[64,1024]{1,0:T(8,128)(2,1)S(1)}, bf16[64,1024]{1,0:T(8,128)(2,1)S(1)}, u32[]{:S(2)}, u32[]{:S(2)}) %collective-permute-start.3) | collective-permute-done | bytes 131104 | tf_op jit(solution)/shard_map/ppermute | solution.py:35
  21.0 0.0 collective-permute-done.q_sib
  21.0 0.0 collective-permute-done.1.g_sib
  21.0 0.0 copy-done
  21.0 2.7 %attention_leading.1 = (bf16[2,64,2048]{2,1,0:T(8,128)(2,1)S(1)}, f32[448,1024]{1,0:T(8,128)S(1)}) custom-call(s32[1]{0:T(128)} %bitcast.place, s32[256]{0:T(256)} %slots.7, s32[4,256]{1,0:T(4,128)S(1)} %bitcast.2, s32[4,256]{1,0:T(4,128)S(1)} %get-tuple-element.18.row_start, bf16[128,2048]{1,0:T(8,128)(2,1)S(1)} %get-tuple-element.19.q_own, ...), custom_call_target="tpu_custom_call" | custom-call | flops 68719476736 | bytes 4194304 | tf_op jit(solution)/shard_map/attention_leading/pallas_call | solution.py:453
  23.7 0.8 %collective-permute-done.5.refs_0_ = bf16[64,1024]{1,0:T(8,128)(2,1)S(1)} collective-permute-done((bf16[64,1024]{1,0:T(8,128)(2,1)S(1)}, bf16[64,1024]{1,0:T(8,128)(2,1)S(1)}, u32[]{:S(2)}, u32[]{:S(2)}) %collective-permute-start.5) | collective-permute-done | bytes 131104 | tf_op jit(solution)/shard_map/ppermute | solution.py:35
  24.5 2.9 %attention_last.1 = (bf16[2,64,2048]{2,1,0:T(8,128)(2,1)S(1)}, f32[128,1024]{1,0:T(8,128)S(1)}, bf16[192,2048]{1,0:T(8,128)(2,1)S(1)}, bf16[128,1024]{1,0:T(8,12...) custom-call(s32[1]{0:T(128)} %bitcast.place, s32[256]{0:T(256)} %slots.7, s32[4,256]{1,0:T(4,128)S(1)} %bitcast.3, ...), custom_call_target="tpu_custom_call" | custom-call | tf_op jit(solution)/shard_map/attention_last/pallas_call | solution.py:466
  27.4 0.1 collective-permute-start.6
  27.5 5.4 %collective-permute-start.8 = (bf16[64,1024]{1,0:T(8,128)(2,1)S(1)}, bf16[64,1024]{1,0:T(8,128)(2,1)S(1)}, u32[]{:S(2)}, u32[]{:S(2)}) collective-permute-start(bf16[64,1024]{1,0:T(8,128)(2,1)S(1)} %get-tuple-element.30), channel_id=1, source_target_pairs={{0,127},{1,2},{2,1},{3,4},{4,3},{5,6},{6,5},{7,8},{8,7},{9,10},{10... | collective-permute-start | bytes 393224 | tf_op jit(solution)/shard_map/ppermute | solution.py:35
  32.8 0.8 %collective-permute-start.9 = (bf16[64,1024]{1,0:T(8,128)(2,1)S(1)}, bf16[64,1024]{1,0:T(8,128)(2,1)S(1)}, u32[]{:S(2)}, u32[]{:S(2)}) collective-permute-start(bf16[64,1024]{1,0:T(8,128)(2,1)S(1)} %get-tuple-element.31), channel_id=1, source_target_pairs={{0,125},{1,4},{2,127},{3,6},{4,1},{5,8},{6,3},{7,10},{8,5},{9,12},... | collective-permute-start | bytes 393224 | tf_op jit(solution)/shard_map/ppermute | solution.py:35
  33.6 0.0 collective-permute-start.10
  33.6 1.6 %collective-permute-done.6.back_a = bf16[128,1024]{1,0:T(8,128)(2,1)S(1)} collective-permute-done((bf16[128,1024]{1,0:T(8,128)(2,1)S(1)}, bf16[128,1024]{1,0:T(8,128)(2,1)S(1)}, u32[]{:S(2)}, u32[]{:S(2)}) %collective-permute-start.6) | collective-permute-done | bytes 262176 | tf_op jit(solution)/shard_map/ppermute | solution.py:35
  35.3 1.3 %collective-permute-start.7 = (bf16[64,1024]{1,0:T(8,128)(2,1)S(1)}, bf16[64,1024]{1,0:T(8,128)(2,1)S(1)}, u32[]{:S(2)}, u32[]{:S(2)}) collective-permute-start(bf16[64,1024]{1,0:T(8,128)(2,1)S(1)} %slice_select_fusion), channel_id=1, source_target_pairs={{1,0},{3,2},{5,4},{7,6},{9,8},{11,10},{13,12},{15,14},{17,16},{19,... | collective-permute-start | bytes 393224 | tf_op jit(solution)/shard_map/ppermute | solution.py:35
  36.6 0.8 %two_away_sum.1.own = f32[128,1024]{1,0:T(8,128)S(1)} custom-call(s32[1]{0:T(128)} %bitcast.place, s32[256]{0:T(256)} %slots.7, f32[128,1024]{1,0:T(8,128)S(1)} %get-tuple-element.28.own, bf16[128,1024]{1,0:T(8,128)(2,1)S(1)} %collective-permute-done.6.back_a), custom_call_target="tpu_custom_call" | custom-call | flops 17179869184 | bytes 1048576 | tf_op jit(solution)/shard_map/two_away_sum/pallas_call | solution.py:489
  37.3 0.9 %collective-permute-done.8.back_b = bf16[64,1024]{1,0:T(8,128)(2,1)S(1)} collective-permute-done((bf16[64,1024]{1,0:T(8,128)(2,1)S(1)}, bf16[64,1024]{1,0:T(8,128)(2,1)S(1)}, u32[]{:S(2)}, u32[]{:S(2)}) %collective-permute-start.8) | collective-permute-done | bytes 131104 | tf_op jit(solution)/shard_map/ppermute | solution.py:35
  38.3 4.1 %collective-permute-done.9.back_c = bf16[64,1024]{1,0:T(8,128)(2,1)S(1)} collective-permute-done((bf16[64,1024]{1,0:T(8,128)(2,1)S(1)}, bf16[64,1024]{1,0:T(8,128)(2,1)S(1)}, u32[]{:S(2)}, u32[]{:S(2)}) %collective-permute-start.9) | collective-permute-done | bytes 131104 | tf_op jit(solution)/shard_map/ppermute | solution.py:35
  42.4 0.0 collective-permute-done.7.lent
  42.4 0.0 collective-permute-done.10.theirs
  42.4 1.6 %gradients_out.1 = (bf16[128,2048]{1,0:T(8,128)(2,1)}, bf16[128,512]{1,0:T(8,128)(2,1)}, bf16[128,512]{1,0:T(8,128)(2,1)}) custom-call(s32[1]{0:T(128)} %bitcast.place, s32[256]{0:T(256)} %slots.7, s32[4,256]{1,0:T(4,128)S(1)} %bitcast.4, bf16[2,64,2048]{2,1,0:T(8,128)(2,1)S(1)} %get-tuple-element.27.mine, f32[128,1024]{1,0:T(8,128)S(1)} %two_away_sum.1.own, ...), custom_call_target="tpu_custom_call" | custom-call | tf_op jit(solution)/shard_map/gradients_out/pallas_call | solution.py:501
  (1 shorter events, 0.0 us)
Async XLA Ops:
  0.6 20.3 %copy-start = (s32[256,4]{0,1:T(4,128)S(1)}, s32[256,4]{0,1:T(4,128)}, u32[]{:S(2)}) copy-start(s32[256,4]{0,1:T(4,128)} %param.13) | copy-start | bytes 12292
  0.6 20.3 %collective-permute-start = (bf16[128,2048]{1,0:T(8,128)(2,1)}, bf16[128,2048]{1,0:T(8,128)(2,1)S(1)}, u32[]{:S(2)}, u32[]{:S(2)}) collective-permute-start(bf16[128,2048]{1,0:T(8,128)(2,1)} %queries.1), channel_id=1, source_target_pairs={{0,1},{1,0},{2,3},{3,2},{4,5},{5,4},{6,7},{7,6},{8,9},{9,8},{10,11... | collective-permute-start | bytes 1572872 | tf_op jit(solution)/shard_map/ppermute | solution.py:35
  0.7 20.2 %collective-permute-start.1 = (bf16[128,2048]{1,0:T(8,128)(2,1)}, bf16[128,2048]{1,0:T(8,128)(2,1)S(1)}, u32[]{:S(2)}, u32[]{:S(2)}) collective-permute-start(bf16[128,2048]{1,0:T(8,128)(2,1)} %grads.1), channel_id=1, source_target_pairs={{0,1},{1,0},{2,3},{3,2},{4,5},{5,4},{6,7},{7,6},{8,9},{9,8},{10,11... | collective-permute-start | bytes 1572872 | tf_op jit(solution)/shard_map/ppermute | solution.py:35
  2.8 12.3 %collective-permute-start.2 = (bf16[128,1024]{1,0:T(8,128)(2,1)S(1)}, bf16[128,1024]{1,0:T(8,128)(2,1)S(1)}, u32[]{:S(2)}, u32[]{:S(2)}) collective-permute-start(bf16[128,1024]{1,0:T(8,128)(2,1)S(1)} %get-tuple-element.21.kv_own), channel_id=1, source_target_pairs={{0,1},{1,0},{2,3},{3,2},{4,5},{5,4},{6,7},{7,6},{8,9},{9,8},{10,11... | collective-permute-start | bytes 786440 | tf_op jit(solution)/shard_map/ppermute | solution.py:35
  3.0 12.1 %collective-permute-start.4 = (bf16[64,1024]{1,0:T(8,128)(2,1)S(1)}, bf16[64,1024]{1,0:T(8,128)(2,1)S(1)}, u32[]{:S(2)}, u32[]{:S(2)}) collective-permute-start(bf16[64,1024]{1,0:T(8,128)(2,1)S(1)} %get-tuple-element.23), channel_id=1, source_target_pairs={{0,127},{1,2},{2,1},{3,4},{4,3},{5,6},{6,5},{7,8},{8,7},{9,10},{10... | collective-permute-start | bytes 393224 | tf_op jit(solution)/shard_map/ppermute | solution.py:35
  11.8 9.2 %collective-permute-start.3 = (bf16[64,1024]{1,0:T(8,128)(2,1)S(1)}, bf16[64,1024]{1,0:T(8,128)(2,1)S(1)}, u32[]{:S(2)}, u32[]{:S(2)}) collective-permute-start(bf16[64,1024]{1,0:T(8,128)(2,1)S(1)} %get-tuple-element.22), channel_id=1, source_target_pairs={{0,2},{1,127},{2,4},{3,1},{4,6},{5,3},{6,8},{7,5},{8,10},{9,7},{10... | collective-permute-start | bytes 393224 | tf_op jit(solution)/shard_map/ppermute | solution.py:35
  15.2 9.3 %collective-permute-start.5 = (bf16[64,1024]{1,0:T(8,128)(2,1)S(1)}, bf16[64,1024]{1,0:T(8,128)(2,1)S(1)}, u32[]{:S(2)}, u32[]{:S(2)}) collective-permute-start(bf16[64,1024]{1,0:T(8,128)(2,1)S(1)} %compare_select_fusion), channel_id=1, source_target_pairs={{0,2},{1,127},{2,4},{3,1},{4,6},{5,3},{6,8},{7,5},{8,10},{9,7},{10... | collective-permute-start | bytes 393224 | tf_op jit(solution)/shard_map/ppermute | solution.py:35
  27.4 7.9 %collective-permute-start.6 = (bf16[128,1024]{1,0:T(8,128)(2,1)S(1)}, bf16[128,1024]{1,0:T(8,128)(2,1)S(1)}, u32[]{:S(2)}, u32[]{:S(2)}) collective-permute-start(bf16[128,1024]{1,0:T(8,128)(2,1)S(1)} %get-tuple-element.29), channel_id=1, source_target_pairs={{0,126},{1,3},{2,0},{3,5},{4,2},{5,7},{6,4},{7,9},{8,6},{9,11},{10... | collective-permute-start | bytes 786440 | tf_op jit(solution)/shard_map/ppermute | solution.py:35
  27.5 10.8 %collective-permute-start.8 = (bf16[64,1024]{1,0:T(8,128)(2,1)S(1)}, bf16[64,1024]{1,0:T(8,128)(2,1)S(1)}, u32[]{:S(2)}, u32[]{:S(2)}) collective-permute-start(bf16[64,1024]{1,0:T(8,128)(2,1)S(1)} %get-tuple-element.30), channel_id=1, source_target_pairs={{0,127},{1,2},{2,1},{3,4},{4,3},{5,6},{6,5},{7,8},{8,7},{9,10},{10... | collective-permute-start | bytes 393224 | tf_op jit(solution)/shard_map/ppermute | solution.py:35
  32.8 9.5 %collective-permute-start.9 = (bf16[64,1024]{1,0:T(8,128)(2,1)S(1)}, bf16[64,1024]{1,0:T(8,128)(2,1)S(1)}, u32[]{:S(2)}, u32[]{:S(2)}) collective-permute-start(bf16[64,1024]{1,0:T(8,128)(2,1)S(1)} %get-tuple-element.31), channel_id=1, source_target_pairs={{0,125},{1,4},{2,127},{3,6},{4,1},{5,8},{6,3},{7,10},{8,5},{9,12},... | collective-permute-start | bytes 393224 | tf_op jit(solution)/shard_map/ppermute | solution.py:35
  33.6 8.7 %collective-permute-start.10 = (bf16[192,2048]{1,0:T(8,128)(2,1)S(1)}, bf16[192,2048]{1,0:T(8,128)(2,1)S(1)}, u32[]{:S(2)}, u32[]{:S(2)}) collective-permute-start(bf16[192,2048]{1,0:T(8,128)(2,1)S(1)} %get-tuple-element.32), channel_id=1, source_target_pairs={{0,1},{1,0},{2,3},{3,2},{4,5},{5,4},{6,7},{7,6},{8,9},{9,8},{10,11... | collective-permute-start | bytes 2359304 | tf_op jit(solution)/shard_map/ppermute | solution.py:35
  35.3 7.1 %collective-permute-start.7 = (bf16[64,1024]{1,0:T(8,128)(2,1)S(1)}, bf16[64,1024]{1,0:T(8,128)(2,1)S(1)}, u32[]{:S(2)}, u32[]{:S(2)}) collective-permute-start(bf16[64,1024]{1,0:T(8,128)(2,1)S(1)} %slice_select_fusion), channel_id=1, source_target_pairs={{1,0},{3,2},{5,4},{7,6},{9,8},{11,10},{13,12},{15,14},{17,16},{19,... | collective-permute-start | bytes 393224 | tf_op jit(solution)/shard_map/ppermute | solution.py:35

commit v2 on v1

--- a/solution.py
+++ b/solution.py
@@ -309,20 +309,15 @@
         copy.wait()
 
 
-def near_kernel(place, slots, own, back_a, out):
+def far_kernel(place, own, back_c, out):
     parity = lax.rem(place[0], 2)
-    is_odd = parity == 1
-    own_rows = pl.ds(pl.multiple_of(parity * ROWS, ROWS), ROWS)
     out[...] = own[...]
-    out[own_rows, :] += back_a[:ROWS, :].astype(jnp.float32)
-    holder = slots[2 * (place[0] - parity) + 2] == slots.shape[0] // 2 - 1
-
-    @pl.when(jnp.logical_and(is_odd, holder))
-    def _():
-        out[:ROWS, :] += back_a[ROWS:, :].astype(jnp.float32)
-
-
-def final_kernel(place, slots, live, mine, own, lent, back_b, back_c, theirs, *outs):
+    out[pl.ds(pl.multiple_of((1 - parity) * ROWS, ROWS), ROWS), :] += back_c[...].astype(
+        jnp.float32
+    )
+
+
+def final_kernel(place, slots, live, mine, own, lent, back_b, back_a, theirs, *outs):
     query_out, key_out, value_out = outs
     me = place[0]
     parity = lax.rem(me, 2)
@@ -349,15 +344,18 @@
     def _():
         query_out[other_rows, :] = theirs[:ROWS, :]
 
+    keeps = jnp.logical_and(is_odd, slots[chip_base + 2] == slots.shape[0] // 2 - 1)
+    kept = jnp.where(keeps, 1.0, 0.0)
     f32 = jnp.float32
     for out, first in ((key_out, 0), (value_out, KV)):
         columns = slice(first, first + KV)
-        cross = back_b[:, columns].astype(f32) + back_c[:, columns].astype(f32)
+        chain = back_a[:ROWS, columns].astype(f32)
+        cross = back_b[:, columns].astype(f32)
         low = own[:ROWS, columns] + theirs[2 * ROWS :, columns].astype(f32)
-        low = low + lent[:, columns].astype(f32) + jnp.where(is_odd, cross, 0.0)
+        low = low + lent[:, columns].astype(f32) + kept * back_a[ROWS:, columns].astype(f32)
         high = own[ROWS:, columns] + theirs[2 * ROWS :, 2 * KV + first : 3 * KV + first].astype(f32)
-        out[:ROWS, :] = low.astype(out.dtype)
-        out[ROWS:, :] = (high + jnp.where(is_odd, 0.0, cross)).astype(out.dtype)
+        out[:ROWS, :] = (low + jnp.where(is_odd, cross, chain)).astype(out.dtype)
+        out[ROWS:, :] = (high + jnp.where(is_odd, chain, cross)).astype(out.dtype)
 
 
 def vmem(count):
@@ -484,19 +482,21 @@
     back_c = send(out_c, -3, 3)
     back_b = send(out_b, -1, 1)
     back_sib = send(out_sib, 1, -1)
-    lent = send(jnp.where(fold == 2, back_a[ROWS:], 0), None, -1)
 
     own = pl.pallas_call(
-        near_kernel,
+        far_kernel,
         out_shape=wide,
-        in_specs=smem(2) + vmem(2),
+        in_specs=smem(1) + vmem(2),
         out_specs=vmem(1)[0],
         compiler_params=params,
         cost_estimate=pl.CostEstimate(
             flops=NEAR_COST, bytes_accessed=1 << 20, transcendentals=0
         ),
-        name="two_away_sum",
-    )(place, in_hbm(slot_to_block), own, back_a)
+        name="three_away_sum",
+    )(place, own, back_c)
+
+    own, back_a = lax.optimization_barrier((own, back_a))
+    lent = send(jnp.where(fold == 2, back_a[ROWS:], 0), None, -1)
 
     query_grad, key_gradient, value_gradient = pl.pallas_call(
         final_kernel,
@@ -514,7 +514,7 @@
         own,
         lent,
         back_b,
-        back_c,
+        back_a,
         back_sib,
     )
     return query_grad, key_gradient, value_gradient

time: 44.2 us -> 48.9 us (1.11)
  the two profiles are of different devices: /device:TPU:16 before, /device:TPU:1 now
where the time goes in v2:
time: 48.9 us; the launch traced here: 48.7 us
  starting transfers between devices  30 us (61%)
  waiting for transfers between devices  8.96 us (18%)
  Pallas kernels  8.89 us (18%)
  between operations  0.73 us (1%)
    ppermute x11, starting transfers between devices, send(): return lax.ppermute(array, 'ctx', pairs)  30 us
    ppermute x11, waiting for transfers between devices, send(): return lax.ppermute(array, 'ctx', pairs)  8.96 us
    pallas_call x1, Pallas kernels, shards(): pl.pallas_call(functools.partial(attention_kernel, False), out_shape=(bf1...  2.94 us
    pallas_call x1, Pallas kernels, shards(): pl.pallas_call(functools.partial(attention_kernel, True), out_shape=(bf16...  2.7 us
    pallas_call x1, Pallas kernels, shards(): pl.pallas_call(final_kernel, out_shape=(bf16((2 * ROWS, WIDE)), bf16((2 *...  1.63 us
    pallas_call x1, Pallas kernels, shards(): pl.pallas_call(pack_kernel, out_shape=(bf16((2 * ROWS, 2 * KV)), bf16((RO...  1.56 us
  transfers between devices with their start and end apart: 11, of which 2 were waited for; matrix products, arithmetic and copies ran while one was open for 0% of the time, Pallas kernels for 9%

profile of v2, /device:TPU:1, one launch (start us, length us, event | category | flops | bytes accessed | tf_op | source)
XLA Modules:
  0.0 48.7 jit_solution(18412434533275234865)
XLA Ops:
  0.6 0.0 copy-start
  0.6 3.3 %collective-permute-start = (bf16[128,2048]{1,0:T(8,128)(2,1)}, bf16[128,2048]{1,0:T(8,128)(2,1)S(1)}, u32[]{:S(2)}, u32[]{:S(2)}) collective-permute-start(bf16[128,2048]{1,0:T(8,128)(2,1)} %queries.1), channel_id=1, source_target_pairs={{0,1},{1,0},{2,3},{3,2},{4,5},{5,4},{6,7},{7,6},{8,9},{9,8},{10,11... | collective-permute-start | bytes 1572872 | tf_op jit(solution)/shard_map/ppermute | solution.py:35
  4.0 0.1 collective-permute-start.1
  4.1 1.6 %prepare.1 = (bf16[128,1024]{1,0:T(8,128)(2,1)S(1)}, bf16[64,1024]{1,0:T(8,128)(2,1)S(1)}, bf16[64,1024]{1,0:T(8,128)(2,1)S(1)}, bf16[128,2048]{1,0:T(8,128)(2,1...) custom-call(s32[1]{0:T(128)} %bitcast.place, s32[256]{0:T(256)} %slots.5, ...), custom_call_target="tpu_custom_call" | custom-call | tf_op jit(solution)/shard_map/prepare/pallas_call | solution.py:392
  5.6 0.5 %collective-permute-start.2 = (bf16[128,1024]{1,0:T(8,128)(2,1)S(1)}, bf16[128,1024]{1,0:T(8,128)(2,1)S(1)}, u32[]{:S(2)}, u32[]{:S(2)}) collective-permute-start(bf16[128,1024]{1,0:T(8,128)(2,1)S(1)} %get-tuple-element.23.kv_own), channel_id=1, source_target_pairs={{0,1},{1,0},{2,3},{3,2},{4,5},{5,4},{6,7},{7,6},{8,9},{9,8},{10,11... | collective-permute-start | bytes 786440 | tf_op jit(solution)/shard_map/ppermute | solution.py:35
  6.1 0.0 collective-permute-start.4
  6.1 7.1 %collective-permute-start.3 = (bf16[64,1024]{1,0:T(8,128)(2,1)S(1)}, bf16[64,1024]{1,0:T(8,128)(2,1)S(1)}, u32[]{:S(2)}, u32[]{:S(2)}) collective-permute-start(bf16[64,1024]{1,0:T(8,128)(2,1)S(1)} %get-tuple-element.24), channel_id=1, source_target_pairs={{0,2},{1,127},{2,4},{3,1},{4,6},{5,3},{6,8},{7,5},{8,10},{9,7},{10... | collective-permute-start | bytes 393224 | tf_op jit(solution)/shard_map/ppermute | solution.py:35
  13.2 0.0 collective-permute-done.4.kv_b
  13.2 0.0 collective-permute-done.2.kv_sib
  13.2 0.1 compare_select_fusion
  13.3 9.5 %collective-permute-start.5 = (bf16[64,1024]{1,0:T(8,128)(2,1)S(1)}, bf16[64,1024]{1,0:T(8,128)(2,1)S(1)}, u32[]{:S(2)}, u32[]{:S(2)}) collective-permute-start(bf16[64,1024]{1,0:T(8,128)(2,1)S(1)} %compare_select_fusion), channel_id=1, source_target_pairs={{0,2},{1,127},{2,4},{3,1},{4,6},{5,3},{6,8},{7,5},{8,10},{9,7},{10... | collective-permute-start | bytes 393224 | tf_op jit(solution)/shard_map/ppermute | solution.py:35
  22.8 0.0 collective-permute-done.3.kv_a
  22.8 0.0 collective-permute-done.q_sib
  22.8 0.0 collective-permute-done.1.g_sib
  22.8 0.0 copy-done
  22.8 2.7 %attention_leading.1 = (bf16[2,64,2048]{2,1,0:T(8,128)(2,1)S(1)}, f32[448,1024]{1,0:T(8,128)S(1)}) custom-call(s32[1]{0:T(128)} %bitcast.place, s32[256]{0:T(256)} %slots.5, s32[4,256]{1,0:T(4,128)S(1)} %bitcast.2, s32[4,256]{1,0:T(4,128)S(1)} %get-tuple-element.20.row_start, bf16[128,2048]{1,0:T(8,128)(2,1)S(1)} %get-tuple-element.21.q_own, ...), custom_call_target="tpu_custom_call" | custom-call | flops 68719476736 | bytes 4194304 | tf_op jit(solution)/shard_map/attention_leading/pallas_call | solution.py:451
  25.5 0.0 collective-permute-done.5.refs_0_
  25.6 2.9 %attention_last.1 = (bf16[2,64,2048]{2,1,0:T(8,128)(2,1)S(1)}, f32[128,1024]{1,0:T(8,128)S(1)}, bf16[192,2048]{1,0:T(8,128)(2,1)S(1)}, bf16[128,1024]{1,0:T(8,12...) custom-call(s32[1]{0:T(128)} %bitcast.place, s32[256]{0:T(256)} %slots.5, s32[4,256]{1,0:T(4,128)S(1)} %bitcast.3, ...), custom_call_target="tpu_custom_call" | custom-call | tf_op jit(solution)/shard_map/attention_last/pallas_call | solution.py:464
  28.5 0.1 collective-permute-start.6
  28.6 6.7 %collective-permute-start.9 = (bf16[64,1024]{1,0:T(8,128)(2,1)S(1)}, bf16[64,1024]{1,0:T(8,128)(2,1)S(1)}, u32[]{:S(2)}, u32[]{:S(2)}) collective-permute-start(bf16[64,1024]{1,0:T(8,128)(2,1)S(1)} %get-tuple-element.35), channel_id=1, source_target_pairs={{0,127},{1,2},{2,1},{3,4},{4,3},{5,6},{6,5},{7,8},{8,7},{9,10},{10... | collective-permute-start | bytes 393224 | tf_op jit(solution)/shard_map/ppermute | solution.py:35
  35.3 0.0 collective-permute-start.7
  35.3 1.4 %collective-permute-start.10 = (bf16[192,2048]{1,0:T(8,128)(2,1)S(1)}, bf16[192,2048]{1,0:T(8,128)(2,1)S(1)}, u32[]{:S(2)}, u32[]{:S(2)}) collective-permute-start(bf16[192,2048]{1,0:T(8,128)(2,1)S(1)} %get-tuple-element.36), channel_id=1, source_target_pairs={{0,1},{1,0},{2,3},{3,2},{4,5},{5,4},{6,7},{7,6},{8,9},{9,8},{10,11... | collective-permute-start | bytes 2359304 | tf_op jit(solution)/shard_map/ppermute | solution.py:35
  36.7 0.0 collective-permute-done.6.back_c
  36.7 0.1 three_away_sum.1.own
  36.8 8.0 %collective-permute-done.7.back_a = bf16[128,1024]{1,0:T(8,128)(2,1)S(1)} collective-permute-done((bf16[128,1024]{1,0:T(8,128)(2,1)S(1)}, bf16[128,1024]{1,0:T(8,128)(2,1)S(1)}, u32[]{:S(2)}, u32[]{:S(2)}) %collective-permute-start.7) | collective-permute-done | bytes 262176 | tf_op jit(solution)/shard_map/ppermute | solution.py:35
  44.8 1.3 %collective-permute-start.8 = (bf16[64,1024]{1,0:T(8,128)(2,1)S(1)}, bf16[64,1024]{1,0:T(8,128)(2,1)S(1)}, u32[]{:S(2)}, u32[]{:S(2)}) collective-permute-start(bf16[64,1024]{1,0:T(8,128)(2,1)S(1)} %slice_select_fusion.1), channel_id=1, source_target_pairs={{1,0},{3,2},{5,4},{7,6},{9,8},{11,10},{13,12},{15,14},{17,16},{19,... | collective-permute-start | bytes 393224 | tf_op jit(solution)/shard_map/ppermute | solution.py:35
  46.1 0.0 collective-permute-done.9.back_b
  46.1 1.0 %collective-permute-done.8.lent = bf16[64,1024]{1,0:T(8,128)(2,1)S(1)} collective-permute-done((bf16[64,1024]{1,0:T(8,128)(2,1)S(1)}, bf16[64,1024]{1,0:T(8,128)(2,1)S(1)}, u32[]{:S(2)}, u32[]{:S(2)}) %collective-permute-start.8) | collective-permute-done | bytes 131104 | tf_op jit(solution)/shard_map/ppermute | solution.py:35
  47.1 0.0 collective-permute-done.10.theirs
  47.1 1.6 %gradients_out.1 = (bf16[128,2048]{1,0:T(8,128)(2,1)}, bf16[128,512]{1,0:T(8,128)(2,1)}, bf16[128,512]{1,0:T(8,128)(2,1)}) custom-call(s32[1]{0:T(128)} %bitcast.place, s32[256]{0:T(256)} %slots.5, s32[4,256]{1,0:T(4,128)S(1)} %bitcast.4, bf16[2,64,2048]{2,1,0:T(8,128)(2,1)S(1)} %get-tuple-element.29.mine, f32[128,1024]{1,0:T(8,128)S(1)} %three_away_sum.1.own, ...), custom_call_target="tpu_custom_call" | custom-call | tf_op jit(solution)/shard_map/gradients_out/pallas_call | solution.py:501
  (1 shorter events, 0.0 us)
Async XLA Ops:
  0.6 22.2 %copy-start = (s32[256,4]{0,1:T(4,128)S(1)}, s32[256,4]{0,1:T(4,128)}, u32[]{:S(2)}) copy-start(s32[256,4]{0,1:T(4,128)} %param.13) | copy-start | bytes 12292
  0.6 22.2 %collective-permute-start = (bf16[128,2048]{1,0:T(8,128)(2,1)}, bf16[128,2048]{1,0:T(8,128)(2,1)S(1)}, u32[]{:S(2)}, u32[]{:S(2)}) collective-permute-start(bf16[128,2048]{1,0:T(8,128)(2,1)} %queries.1), channel_id=1, source_target_pairs={{0,1},{1,0},{2,3},{3,2},{4,5},{5,4},{6,7},{7,6},{8,9},{9,8},{10,11... | collective-permute-start | bytes 1572872 | tf_op jit(solution)/shard_map/ppermute | solution.py:35
  4.0 18.9 %collective-permute-start.1 = (bf16[128,2048]{1,0:T(8,128)(2,1)}, bf16[128,2048]{1,0:T(8,128)(2,1)S(1)}, u32[]{:S(2)}, u32[]{:S(2)}) collective-permute-start(bf16[128,2048]{1,0:T(8,128)(2,1)} %grads.1), channel_id=1, source_target_pairs={{0,1},{1,0},{2,3},{3,2},{4,5},{5,4},{6,7},{7,6},{8,9},{9,8},{10,11... | collective-permute-start | bytes 1572872 | tf_op jit(solution)/shard_map/ppermute | solution.py:35
  5.6 7.6 %collective-permute-start.2 = (bf16[128,1024]{1,0:T(8,128)(2,1)S(1)}, bf16[128,1024]{1,0:T(8,128)(2,1)S(1)}, u32[]{:S(2)}, u32[]{:S(2)}) collective-permute-start(bf16[128,1024]{1,0:T(8,128)(2,1)S(1)} %get-tuple-element.23.kv_own), channel_id=1, source_target_pairs={{0,1},{1,0},{2,3},{3,2},{4,5},{5,4},{6,7},{7,6},{8,9},{9,8},{10,11... | collective-permute-start | bytes 786440 | tf_op jit(solution)/shard_map/ppermute | solution.py:35
  6.1 7.1 %collective-permute-start.4 = (bf16[64,1024]{1,0:T(8,128)(2,1)S(1)}, bf16[64,1024]{1,0:T(8,128)(2,1)S(1)}, u32[]{:S(2)}, u32[]{:S(2)}) collective-permute-start(bf16[64,1024]{1,0:T(8,128)(2,1)S(1)} %get-tuple-element.25), channel_id=1, source_target_pairs={{0,127},{1,2},{2,1},{3,4},{4,3},{5,6},{6,5},{7,8},{8,7},{9,10},{10... | collective-permute-start | bytes 393224 | tf_op jit(solution)/shard_map/ppermute | solution.py:35
  6.1 16.7 %collective-permute-start.3 = (bf16[64,1024]{1,0:T(8,128)(2,1)S(1)}, bf16[64,1024]{1,0:T(8,128)(2,1)S(1)}, u32[]{:S(2)}, u32[]{:S(2)}) collective-permute-start(bf16[64,1024]{1,0:T(8,128)(2,1)S(1)} %get-tuple-element.24), channel_id=1, source_target_pairs={{0,2},{1,127},{2,4},{3,1},{4,6},{5,3},{6,8},{7,5},{8,10},{9,7},{10... | collective-permute-start | bytes 393224 | tf_op jit(solution)/shard_map/ppermute | solution.py:35
  13.3 12.2 %collective-permute-start.5 = (bf16[64,1024]{1,0:T(8,128)(2,1)S(1)}, bf16[64,1024]{1,0:T(8,128)(2,1)S(1)}, u32[]{:S(2)}, u32[]{:S(2)}) collective-permute-start(bf16[64,1024]{1,0:T(8,128)(2,1)S(1)} %compare_select_fusion), channel_id=1, source_target_pairs={{0,2},{1,127},{2,4},{3,1},{4,6},{5,3},{6,8},{7,5},{8,10},{9,7},{10... | collective-permute-start | bytes 393224 | tf_op jit(solution)/shard_map/ppermute | solution.py:35
  28.5 8.2 %collective-permute-start.6 = (bf16[64,1024]{1,0:T(8,128)(2,1)S(1)}, bf16[64,1024]{1,0:T(8,128)(2,1)S(1)}, u32[]{:S(2)}, u32[]{:S(2)}) collective-permute-start(bf16[64,1024]{1,0:T(8,128)(2,1)S(1)} %get-tuple-element.31), channel_id=1, source_target_pairs={{0,125},{1,4},{2,127},{3,6},{4,1},{5,8},{6,3},{7,10},{8,5},{9,12},... | collective-permute-start | bytes 393224 | tf_op jit(solution)/shard_map/ppermute | solution.py:35
  28.6 17.5 %collective-permute-start.9 = (bf16[64,1024]{1,0:T(8,128)(2,1)S(1)}, bf16[64,1024]{1,0:T(8,128)(2,1)S(1)}, u32[]{:S(2)}, u32[]{:S(2)}) collective-permute-start(bf16[64,1024]{1,0:T(8,128)(2,1)S(1)} %get-tuple-element.35), channel_id=1, source_target_pairs={{0,127},{1,2},{2,1},{3,4},{4,3},{5,6},{6,5},{7,8},{8,7},{9,10},{10... | collective-permute-start | bytes 393224 | tf_op jit(solution)/shard_map/ppermute | solution.py:35
  35.3 9.4 %collective-permute-start.7 = (bf16[128,1024]{1,0:T(8,128)(2,1)S(1)}, bf16[128,1024]{1,0:T(8,128)(2,1)S(1)}, u32[]{:S(2)}, u32[]{:S(2)}) collective-permute-start(bf16[128,1024]{1,0:T(8,128)(2,1)S(1)} %get-tuple-element.32), channel_id=1, source_target_pairs={{0,126},{1,3},{2,0},{3,5},{4,2},{5,7},{6,4},{7,9},{8,6},{9,11},{10... | collective-permute-start | bytes 786440 | tf_op jit(solution)/shard_map/ppermute | solution.py:35
  35.3 11.8 %collective-permute-start.10 = (bf16[192,2048]{1,0:T(8,128)(2,1)S(1)}, bf16[192,2048]{1,0:T(8,128)(2,1)S(1)}, u32[]{:S(2)}, u32[]{:S(2)}) collective-permute-start(bf16[192,2048]{1,0:T(8,128)(2,1)S(1)} %get-tuple-element.36), channel_id=1, source_target_pairs={{0,1},{1,0},{2,3},{3,2},{4,5},{5,4},{6,7},{7,6},{8,9},{9,8},{10,11... | collective-permute-start | bytes 2359304 | tf_op jit(solution)/shard_map/ppermute | solution.py:35
  44.8 2.3 %collective-permute-start.8 = (bf16[64,1024]{1,0:T(8,128)(2,1)S(1)}, bf16[64,1024]{1,0:T(8,128)(2,1)S(1)}, u32[]{:S(2)}, u32[]{:S(2)}) collective-permute-start(bf16[64,1024]{1,0:T(8,128)(2,1)S(1)} %slice_select_fusion.1), channel_id=1, source_target_pairs={{1,0},{3,2},{5,4},{7,6},{9,8},{11,10},{13,12},{15,14},{17,16},{19,... | collective-permute-start | bytes 393224 | tf_op jit(solution)/shard_map/ppermute | solution.py:35
